TPU v7x, 32 devices: a whole 2x2x4 slice. The times are simulated.
32 devices in a mesh: groups: 2 (over y), dp: 4 (over z), tensor: 2 (over x), seq: 2 (over core).
Axes of the slice: x: 2, y: 2, z: 4, core: 2. Of those that a mesh axis runs over, the one named last changes fastest.
Arguments:
- cache: bfloat16 [8, 2, 8, 256, 1024], P(('groups', 'dp'), None, 'seq', None, 'tensor'), parts along dimension 0, may hold values from -6 to 6
- query: bfloat16 [8, 2, 8192], P(('groups', 'dp'), None, 'tensor'), parts along dimension 0
- fresh_key_values: bfloat16 [8, 2, 2, 1024], P(('groups', 'dp'), None, None, 'tensor'), parts along dimension 0, may hold values from -6 to 6
- parents: int32 [8], P('groups'), parts along dimension 0, may hold values from 0 to 3
- lengths: int32 [8], P('groups'), parts along dimension 0, may hold values from 512 to 2048
- page_table: int32 [8, 8], P('groups'), parts along dimension 0, may hold values from 0 to 7, as said below
- out_weight: bfloat16 [8192, 8192], P('tensor', ('dp', 'seq')), may hold values from -0.0625 to 0.0625
Outputs:
- moved_cache: bfloat16 [8, 2, 8, 256, 1024], P(('groups', 'dp'), None, 'seq', None, 'tensor'), parts along dimension 0
- projected: bfloat16 [16, 8192], P(('groups', 'tensor'), ('dp', 'seq')), parts along dimension 0
There are 2 independent parts, one for each index of `groups`. A program takes and returns all parts, laid end to end along the dimension named above; an argument that names none is the same for every part. Nothing has to cross between parts.
Inputs may be any that keep to these rules, and one draw needn't show every extreme that they name: `page_table`: every row is a permutation of the storage slots 0 to 7.
All inputs are finite; a program needn't handle non-finite values.
Results may differ from a plain program's by a relative error of at most 0.009.
Values may be sent and summed in bfloat16 or wider, within the bound.
A program may use at most 64 MiB of HBM per device.

v0:
```python
import math

import jax
import jax.numpy as jnp
from jax import lax
from jax.sharding import PartitionSpec as P

HEAD_SIZE = 128


NEG_FILL = -1e30


def joined(shard, axis, combine):
    everything = jax.tree.map(lambda part: lax.all_gather(part, axis), shard)
    first = jax.tree.map(lambda part: part[0], everything)

    def step(k, so_far):
        return combine(so_far, jax.tree.map(lambda part: part[k], everything))

    return lax.fori_loop(1, lax.axis_size(axis), step, first)


def merge_parts(first, second):
    max_first, total_first, weighted_first = first
    max_second, total_second, weighted_second = second
    max_joint = jnp.maximum(max_first, max_second)
    scale_first = jnp.exp(max_first - max_joint)
    scale_second = jnp.exp(max_second - max_joint)
    return (
        max_joint,
        total_first * scale_first + total_second * scale_second,
        weighted_first * scale_first[..., None] + weighted_second * scale_second[..., None],
    )


def partial_attention(stored_cache, queries, length_caps, page_rows):
    beam_count, _, local_pages, page_len, kv_width = stored_cache.shape
    kv_heads = kv_width // HEAD_SIZE
    new_count = queries.shape[1]
    query_groups = queries.shape[2] // kv_width
    slot_first = lax.axis_index("seq") * local_pages
    slot_ids = slot_first + jnp.arange(local_pages, dtype=jnp.int32)
    page_ids = jnp.arange(page_rows.shape[1], dtype=jnp.int32)
    page_num = jnp.sum(
        page_ids[None, None, :]
        * (page_rows[:, None, :] == slot_ids[None, :, None]).astype(jnp.int32),
        axis=2,
    )
    positions = (
        page_num[:, :, None] * page_len + jnp.arange(page_len, dtype=jnp.int32)[None, None, :]
    )
    in_length = (positions < length_caps[:, None, None]).reshape(beam_count, local_pages * page_len)
    allowed = in_length[:, None, None, None, :]
    cached_key_rows = stored_cache[:, 0].reshape(
        beam_count, local_pages * page_len, kv_heads, HEAD_SIZE
    )
    cached_value_rows = stored_cache[:, 1].reshape(
        beam_count, local_pages * page_len, kv_heads, HEAD_SIZE
    )
    grouped_queries = queries.reshape(beam_count, new_count, kv_heads, query_groups, HEAD_SIZE)
    scores = jnp.einsum(
        "ntkgd,nskd->ntkgs", grouped_queries, cached_key_rows, preferred_element_type=jnp.float32
    ) * (1.0 / math.sqrt(HEAD_SIZE))
    row_max = jnp.max(jnp.where(allowed, scores, NEG_FILL), axis=-1)
    weights = jnp.where(allowed, jnp.exp(scores - row_max[..., None]), 0.0)
    totals = jnp.sum(weights, axis=-1)
    weighted = jnp.einsum(
        "ntkgs,nskd->ntkgd",
        weights,
        cached_value_rows.astype(jnp.float32),
        precision=lax.Precision.HIGHEST,
    )
    return joined((row_max, totals, weighted), "seq", merge_parts)


def finish(merged, queries, new_pairs):
    row_max, totals, weighted = merged
    beam_count, new_count, q_width = queries.shape
    kv_width = new_pairs.shape[-1]
    kv_heads = kv_width // HEAD_SIZE
    query_groups = q_width // kv_width
    grouped_queries = queries.reshape(beam_count, new_count, kv_heads, query_groups, HEAD_SIZE)
    new_keys = new_pairs[:, 0].reshape(beam_count, new_count, kv_heads, HEAD_SIZE)
    new_values = new_pairs[:, 1].reshape(beam_count, new_count, kv_heads, HEAD_SIZE)
    scores = jnp.einsum(
        "ntkgd,nskd->ntkgs", grouped_queries, new_keys, preferred_element_type=jnp.float32
    ) * (1.0 / math.sqrt(HEAD_SIZE))
    causal = (
        jnp.arange(new_count, dtype=jnp.int32)[:, None]
        >= jnp.arange(new_count, dtype=jnp.int32)[None, :]
    )
    allowed = causal[None, :, None, None, :]
    joint_max = jnp.maximum(row_max, jnp.max(jnp.where(allowed, scores, NEG_FILL), axis=-1))
    old_scale = jnp.exp(row_max - joint_max)
    weights = jnp.where(allowed, jnp.exp(scores - joint_max[..., None]), 0.0)
    total_all = totals * old_scale + jnp.sum(weights, axis=-1)
    weighted_all = weighted * old_scale[..., None] + jnp.einsum(
        "ntkgs,nskd->ntkgd",
        weights,
        new_values.astype(jnp.float32),
        precision=lax.Precision.HIGHEST,
    )
    return (
        (weighted_all / total_all[..., None])
        .reshape(beam_count, new_count, q_width)
        .astype(jnp.bfloat16)
    )


def per_device(cache, query, fresh_key_values, parents, lengths, page_table, out_weight):
    beam_dev = cache.shape[0]
    device_here = lax.axis_index("dp")
    own_parents = lax.dynamic_slice_in_dim(parents, device_here * beam_dev, beam_dev)
    own_lengths = jnp.take(lengths, own_parents)
    own_tables = jnp.take(page_table, own_parents, axis=0)
    every_cache = lax.all_gather(cache, "dp", axis=0, tiled=True)
    moved = jnp.take(every_cache, own_parents, axis=0)
    merged = partial_attention(moved, query, own_lengths, own_tables)
    attended = finish(merged, query, fresh_key_values)
    head_rows = attended.reshape(beam_dev * attended.shape[1], attended.shape[2])
    terms = jnp.dot(
        lax.all_gather(head_rows, "dp", axis=0, tiled=True),
        out_weight,
        preferred_element_type=jnp.float32,
    )
    projected = lax.psum_scatter(
        terms.astype(jnp.bfloat16), "tensor", scatter_dimension=0, tiled=True
    )
    return (moved, projected)


def solution(mesh):
    in_specs = (
        P(("groups", "dp"), None, "seq", None, "tensor"),
        P(("groups", "dp"), None, "tensor"),
        P(("groups", "dp"), None, None, "tensor"),
        P("groups"),
        P("groups"),
        P("groups", None),
        P("tensor", ("dp", "seq")),
    )
    out_specs = (
        P(("groups", "dp"), None, "seq", None, "tensor"),
        P(("groups", "tensor"), ("dp", "seq")),
    )
    return jax.shard_map(
        per_device, mesh=mesh, in_specs=in_specs, out_specs=out_specs, check_vma=False
    )
```

profile of v0, /device:TPU:0, one launch (start us, length us, event | category | flops | bytes accessed | tf_op | source)
XLA Modules:
  0.0 211.3 jit_solution(18246372938418693817)
XLA Ops:
  7.2 0.0 copy-start.1
  7.2 0.0 all-gather.6.cloned.1.call-start
  7.2 0.7 all-gather.6.cloned.1.call-update
  7.9 1.2 dynamic_slice.15
  11.1 1.2 dynamic-slice.10
  12.4 1.2 dynamic-slice.11
  14.8 0.7 fusion.26
  15.5 0.2 select_reduce_fusion.1
  15.7 0.9 convolution_multiply_fusion.1
  16.7 0.1 fusion.16
  16.7 0.1 add.92
  16.8 145.1 %all-gather.6.cloned.1.call-done = bf16[4,2,4,256,512]{4,3,2,1,0:T(8,128)(2,1)} async-done(((bf16[1,2,4,256,512]{4,3,2,1,0:T(8,128)(2,1)}), bf16[4,2,4,256,512]{4,3,2,1,0:T(8,128)(2,1)}) %all-gather.6.cloned.1.call-update) | async-done | bytes 8388624 | tf_op jit(solution)/shard_map/all_gather | solution.py:117
  161.9 1.8 dynamic-slice_select_fusion
  163.7 0.0 copy-start
  163.7 1.4 fusion.31
  165.1 2.2 %reshape.354 = bf16[1024,4,128]{2,1,0:T(4,128)(2,1)} reshape(bf16[1,1,4,256,512]{4,3,2,1,0:T(8,128)(2,1)} %get-tuple-element.63) | data formatting | bytes 2097152 | tf_op jit(solution)/shard_map/reshape.16
  167.3 0.0 copy-done.1
  167.3 1.7 select_reduce_fusion
  169.0 0.2 fusion.7
  169.2 1.8 all-gather.2
  171.0 1.8 all-gather.1
  172.8 0.1 fusion.29
  172.9 1.1 reshape.353
  174.0 1.8 convolution_bitcast_fusion.1
  175.9 1.9 all-gather
  177.7 0.0 copy-done.2
  177.8 0.2 fusion.3
  178.0 13.1 %all-gather.3 = bf16[4,2,4096]{2,1,0:T(2,128)(2,1)S(1)} all-gather(bf16[1,2,4096]{2,1,0:T(2,128)(2,1)S(1)} %reshape.447), channel_id=1, replica_groups=mesh['groups'=2,'dp'=4,'tensor'=2,'seq'=2] {'dp'}, dimensions={0}, use_global_device_ids=true | all-gather | bytes 81920 | tf_op jit(solution)/shard_map/all_gather | solution.py:123
  191.2 4.6 %convolution_convert_fusion = bf16[8,1024]{1,0:T(8,128)(2,1)S(1)} fusion(bf16[8,4096]{1,0:T(8,128)(2,1)S(1)} %reshape.448, bf16[4096,1024]{1,0:T(8,128)(2,1)} %param.13), kind=kOutput, calls=%fused_computation.8 | convolution fusion | flops 67117056 | bytes 8470528 | tf_op jit(solution)/shard_map/dot_general | solution.py:122
  195.7 0.0 copy-done
  195.7 8.1 %all-reduce = bf16[8,1024]{1,0:T(8,128)(2,1)S(1)} all-reduce(bf16[8,1024]{1,0:T(8,128)(2,1)S(1)} %convolution_convert_fusion), channel_id=5, replica_groups=mesh['groups'=2,'dp'=4,'tensor'=2,'seq'=2] {'tensor'}, use_global_device_ids=true, to_apply=%region_5.6.clone | all-reduce | flops 8192 | bytes 32768
  203.9 0.6 constant_dynamic-slice_fusion
  (18 shorter events, 0.1 us)
Async XLA Ops:
  7.2 160.1 %copy-start.1 = (bf16[1,2,4096]{2,1,0:T(2,128)(2,1)S(1)}, bf16[1,2,4096]{2,1,0:T(2,128)(2,1)}, u32[]{:S(2)}) copy-start(bf16[1,2,4096]{2,1,0:T(2,128)(2,1)} %param.8) | copy-start | bytes 49156
  7.2 154.8 %all-gather.6.cloned.1.call-start = ((), (), s32[]{:S(2)}) async-start(), calls=%async_computation | async-start | bytes 10485760 | tf_op jit(solution)/shard_map/all_gather | solution.py:117
  15.7 162.0 %copy-start.2 = (bf16[1,2,2,512]{3,2,1,0:T(2,128)(2,1)S(1)}, bf16[1,2,2,512]{3,2,1,0:T(2,128)(2,1)}, u32[]{:S(2)}) copy-start(bf16[1,2,2,512]{3,2,1,0:T(2,128)(2,1)} %param.9) | copy-start | bytes 12292
  163.7 32.0 %copy-start = (bf16[1,2,4,256,512]{4,3,2,1,0:T(8,128)(2,1)}, bf16[1,2,4,256,512]{4,3,2,1,0:T(8,128)(2,1)S(1)}, u32[]{:S(2)}) copy-start(bf16[1,2,4,256,512]{4,3,2,1,0:T(8,128)(2,1)S(1)} %dynamic-slice_select_fusion) | copy-start | bytes 6291460
Sparse Core Ops, SparseCore 0:
  9.6 152.3 all-gather.5
where the time goes:
time: 212 us; the launch traced here: 211 us
  waiting for transfers between devices  146 us (69%)
  blocking collectives  26.7 us (13%)
  between operations  17.3 us (8%)
  matrix products  9.23 us (4%)
  local copies, waits for them, and re-layouts  9.18 us (4%)
  other arithmetic  3.08 us (1%)
    all_gather x1, waiting for transfers between devices, per_device(): every_cache = lax.all_gather(cache, 'dp', axis=0, tiled=True)  145 us
    all_gather x1, blocking collectives, per_device(): lax.all_gather(head_rows, 'dp', axis=0, tiled=True)  13.1 us
    unnamed x1, blocking collectives  8.12 us
    all_gather x3, blocking collectives, joined(): everything = jax.tree.map(lambda part: lax.all_gather(part, axis), shard)  5.43 us
    dot_general x1, matrix products, per_device(): jnp.dot(lax.all_gather(head_rows, 'dp', axis=0, tiled=True), out_weight,...  4.57 us
  transfers between devices with their start and end apart: 1, of which 1 were waited for; matrix products, arithmetic and copies ran while one was open for 3% of the time, Pallas kernels for 0%

commit v1 on v0

--- a/solution.py
+++ b/solution.py
@@ -3,6 +3,8 @@
 import jax
 import jax.numpy as jnp
 from jax import lax
+from jax.experimental import pallas as pl
+from jax.experimental.pallas import tpu as pltpu
 from jax.sharding import PartitionSpec as P
 
 HEAD_SIZE = 128
@@ -130,6 +132,397 @@
     return (moved, projected)
 
 
+MESH = pl.DeviceIdType.MESH
+CHUNKS = 16
+AHEAD = 6
+
+
+def chain_kernel(
+    parents, lengths, tables, qf, cache, weight,
+    moved, spare, second, out,
+    own, from_left, from_right, to_right, to_left, moved_buf, spare_buf, held_weight,
+    q_all, q_rows, part_send, part_recv, att_all, att_full, out_send, out_recv, need_send, need_recv,
+    own_sem, weight_sem, right_send, right_recv, left_send, left_recv, moved_sem, spare_sem,
+    q_send_sem, q_recv_sem, att_send_sem, att_recv_sem, pair_send_sem, pair_recv_sem,
+):
+    me = lax.axis_index("dp")
+    core = lax.axis_index("seq")
+    tens = lax.axis_index("tensor")
+    group = lax.axis_index("groups")
+    beams = 4
+    kv_heads = qf.shape[0]
+    half_heads = kv_heads // 2
+    rows = beams * 16
+    chunk_rows, kv_width = own.shape[1:]
+    page_len = 256
+    local_pages = own.shape[0] * chunk_rows // (2 * page_len)
+    stored = local_pages * page_len
+    mate = {"seq": 1 - core}
+    across = {"tensor": 1 - tens}
+    other_group = {"groups": 1 - group}
+
+    def far(step):
+        return lax.rem(me + step, beams)
+
+    right, left = {"dp": far(1)}, {"dp": far(3)}
+
+    barrier = pltpu.get_barrier_semaphore()
+    for peer in [{"dp": far(1)}, {"dp": far(2)}, {"dp": far(3)}, mate, across, other_group]:
+        pl.semaphore_signal(barrier, inc=1, device_id=peer, device_id_type=MESH)
+
+    load_own = pltpu.make_async_copy(cache, own, own_sem)
+    load_own.start()
+    load_weight = pltpu.make_async_copy(weight, held_weight, weight_sem)
+
+    par = [parents[i] for i in range(beams)]
+    mine = parents[me]
+    low2, low3 = par[2] < 2, par[3] < 2
+    high0, high1 = par[0] > 1, par[1] > 1
+    twice = (low2 & low3 & (par[2] != par[3])) | (high0 & high1 & (par[0] != par[1]))
+    first_right = jnp.where(low3, par[3], par[2])
+    first_left = jnp.where(high0, par[0], par[1])
+    pass_right = jnp.where(me == 1, first_right == 0, par[3] != 2)
+    pass_left = jnp.where(me == 2, first_left == 3, par[0] != 1)
+    spare_left = (me == 1) & (par[2] == 0)
+    spare_right = (me == 2) & (par[1] == 3)
+    take_left, take_right = mine < me, mine > me
+
+    need_send[...] = jnp.full(need_send.shape, jnp.where(twice, 1, 0), jnp.int32)
+    q_all[me] = qf[...]
+    pl.semaphore_wait(barrier, 6)
+
+    def q_copy(step):
+        return pltpu.make_async_remote_copy(
+            src_ref=qf, dst_ref=q_all.at[me], send_sem=q_send_sem.at[step],
+            recv_sem=q_recv_sem.at[me], device_id={"dp": far(step)}, device_id_type=MESH)
+
+    for step in (1, 2, 3):
+        q_copy(step).start()
+    need_copy = pltpu.make_async_remote_copy(
+        src_ref=need_send, dst_ref=need_recv, send_sem=pair_send_sem.at[3],
+        recv_sem=pair_recv_sem.at[3], device_id=other_group, device_id_type=MESH)
+    need_copy.start()
+
+    def right_copy(c, source):
+        return pltpu.make_async_remote_copy(
+            src_ref=source.at[c], dst_ref=from_left.at[c], send_sem=right_send.at[c],
+            recv_sem=right_recv.at[c], device_id=right, device_id_type=MESH)
+
+    def left_copy(c, source):
+        return pltpu.make_async_remote_copy(
+            src_ref=source.at[c], dst_ref=from_right.at[c], send_sem=left_send.at[c],
+            recv_sem=left_recv.at[c], device_id=left, device_id_type=MESH)
+
+    middle = (me == 1) | (me == 2)
+
+    def first_send(c):
+        @pl.when(me == 0)
+        def _():
+            right_copy(c, cache).start()
+
+        @pl.when(me == beams - 1)
+        def _():
+            left_copy(c, cache).start()
+
+    for c in range(AHEAD):
+        first_send(c)
+    load_own.wait()
+    load_weight.start()
+
+    lag_right = jnp.where(me == 1, 0, 1)
+    lag_left = jnp.where(me == 2, 0, 1)
+
+    def serve(s, _):
+        c_right = s - lag_right
+        c_left = s - lag_left
+
+        @pl.when((me > 0) & (c_right >= 0) & (c_right < CHUNKS))
+        def _():
+            right_copy(c_right, to_right).wait_recv()
+
+            @pl.when(middle)
+            def _():
+                to_right[c_right] = jnp.where(pass_right, from_left[c_right], own[c_right])
+                right_copy(c_right, to_right).start()
+
+        @pl.when((me < beams - 1) & (c_left >= 0) & (c_left < CHUNKS))
+        def _():
+            left_copy(c_left, to_left).wait_recv()
+
+            @pl.when(middle)
+            def _():
+                to_left[c_left] = jnp.where(pass_left, from_right[c_left], own[c_left])
+                left_copy(c_left, to_left).start()
+
+        @pl.when(s + AHEAD < CHUNKS)
+        def _():
+            first_send(s + AHEAD)
+
+        @pl.when(s >= 1)
+        def _():
+            c = s - 1
+            moved_buf[c] = jnp.where(
+                take_left, from_left[c], jnp.where(take_right, from_right[c], own[c]))
+            pltpu.make_async_copy(moved_buf.at[c], moved.at[c], moved_sem.at[c]).start()
+
+            @pl.when(middle)
+            def _():
+                spare_buf[c] = jnp.where(
+                    spare_left, from_left[c], jnp.where(spare_right, from_right[c], own[c]))
+                pltpu.make_async_copy(spare_buf.at[c], spare.at[c], spare_sem.at[c]).start()
+
+        return 0
+
+    def serves(lo, hi):
+        lax.fori_loop(lo, hi, serve, 0)
+
+    row_ids = lax.broadcasted_iota(jnp.int32, (rows, 1), 0)
+    row_beam = lax.rem(row_ids, 2 * beams) // 2
+    row_token = lax.rem(row_ids, 2)
+    row_parent = jnp.zeros((rows, 1), jnp.int32)
+    for i in range(beams):
+        row_parent = jnp.where(row_beam == i, par[i], row_parent)
+    slot_ids = lax.broadcasted_iota(jnp.int32, (1, stored), 1)
+    page_base = jnp.zeros((1, stored), jnp.int32)
+    for slot in range(local_pages):
+        page = jnp.int32(0)
+        for j in range(tables.shape[1]):
+            page = page + jnp.where(tables[me, j] == core * local_pages + slot, j, 0)
+        page_base = jnp.where(slot_ids // page_len == slot, page * page_len, page_base)
+    allowed = page_base + lax.rem(slot_ids, page_len) < lengths[me]
+    scale = 1.0 / math.sqrt(HEAD_SIZE)
+
+    def queries_ready():
+        for step in (1, 2, 3):
+            pltpu.make_async_remote_copy(
+                src_ref=qf, dst_ref=q_all.at[far(step)], send_sem=q_send_sem.at[step],
+                recv_sem=q_recv_sem.at[far(step)], device_id={"dp": far(step)},
+                device_id_type=MESH).wait_recv()
+        r = lax.broadcasted_iota(jnp.int32, (rows, rows), 0)
+        col = lax.broadcasted_iota(jnp.int32, (rows, rows), 1)
+        place = lax.rem(r, 2 * beams) // 2 * 16 + r // (2 * beams) * 2 + lax.rem(r, 2)
+        order = jnp.where(place == col, 1.0, 0.0).astype(jnp.bfloat16)
+        for k in range(kv_heads):
+            stacked = jnp.concatenate([q_all[i, k, 0:16, :] for i in range(beams)], axis=0)
+            q_rows[k] = jnp.dot(order, stacked, preferred_element_type=jnp.float32).astype(
+                jnp.bfloat16)
+
+    half = own.shape[0] // 2
+
+    def head(k, store, at):
+        lanes = pl.ds(pl.multiple_of(k * HEAD_SIZE, HEAD_SIZE), HEAD_SIZE)
+        keys = own[0:half, :, lanes].reshape(stored, HEAD_SIZE)
+        values = own[half:2 * half, :, lanes].reshape(stored, HEAD_SIZE)
+        scores = lax.dot_general(
+            q_rows[k], keys, (((1,), (1,)), ((), ())), preferred_element_type=jnp.float32) * scale
+        top = jnp.max(jnp.where(allowed, scores, NEG_FILL), axis=1, keepdims=True)
+        weights = jnp.where(allowed, jnp.exp(scores - top), 0.0)
+        total = jnp.sum(weights, axis=1, keepdims=True)
+        coarse = weights.astype(jnp.bfloat16)
+        fine = (weights - coarse.astype(jnp.float32)).astype(jnp.bfloat16)
+        both = jnp.dot(
+            jnp.concatenate([coarse, fine], axis=0), values, preferred_element_type=jnp.float32)
+        store[at, 0] = both[:rows] + both[rows:]
+        lane = lax.broadcasted_iota(jnp.int32, (rows, HEAD_SIZE), 1)
+        store[at, 1] = jnp.where(lane < 1, top, total)
+
+    part_copy = pltpu.make_async_remote_copy(
+        src_ref=part_send.at[0], dst_ref=part_recv, send_sem=pair_send_sem.at[0],
+        recv_sem=pair_recv_sem.at[0], device_id=mate, device_id_type=MESH)
+
+    def spread(k, first_row):
+        full = jnp.zeros((rows, HEAD_SIZE), jnp.float32)
+        for i in range(beams):
+            block = q_all[i, k, 16:32, :].astype(jnp.float32)[first_row:first_row + 1]
+            full = jnp.where(row_beam == i, block, full)
+        return full
+
+    def att_copy(step):
+        return pltpu.make_async_remote_copy(
+            src_ref=att_all.at[me], dst_ref=att_all.at[me], send_sem=att_send_sem.at[step],
+            recv_sem=att_recv_sem.at[me], device_id={"dp": far(step)}, device_id_type=MESH)
+
+    def merge():
+        part_copy.wait_recv()
+        for at in range(half_heads):
+            k = core * half_heads + at
+            stat_here, stat_there = part_send[1, at, 1], part_recv[at, 1]
+            top_here, top_there = stat_here[:, 0:1], stat_there[:, 0:1]
+            q_here = q_rows[k].astype(jnp.float32)
+            score0 = jnp.sum(q_here * spread(k, 0), axis=1, keepdims=True) * scale
+            score1 = jnp.sum(q_here * spread(k, 1), axis=1, keepdims=True) * scale
+            score1 = jnp.where(row_token == 1, score1, NEG_FILL)
+            top = jnp.maximum(jnp.maximum(top_here, top_there), jnp.maximum(score0, score1))
+            scale_here, scale_there = jnp.exp(top_here - top), jnp.exp(top_there - top)
+            weight0 = jnp.exp(score0 - top)
+            weight1 = jnp.where(row_token == 1, jnp.exp(score1 - top), 0.0)
+            total = (stat_here[:, 1:2] * scale_here + stat_there[:, 1:2] * scale_there
+                     + weight0 + weight1)
+            weighted = (part_send[1, at, 0] * scale_here + part_recv[at, 0] * scale_there
+                        + weight0 * spread(k, 2) + weight1 * spread(k, 3))
+            att_all[me, at] = (weighted / total).astype(jnp.bfloat16)
+        for step in (1, 2, 3):
+            att_copy(step).start()
+
+    mate_copy = pltpu.make_async_remote_copy(
+        src_ref=att_full.at[core], dst_ref=att_full.at[core], send_sem=pair_send_sem.at[1],
+        recv_sem=pair_recv_sem.at[1], device_id=mate, device_id_type=MESH)
+    mate_wait = pltpu.make_async_remote_copy(
+        src_ref=att_full.at[1 - core], dst_ref=att_full.at[1 - core],
+        send_sem=pair_send_sem.at[1],
+        recv_sem=pair_recv_sem.at[1], device_id=mate, device_id_type=MESH)
+
+    def pick():
+        for step in (1, 2, 3):
+            pltpu.make_async_remote_copy(
+                src_ref=att_all.at[me], dst_ref=att_all.at[far(step)],
+                send_sem=att_send_sem.at[step], recv_sem=att_recv_sem.at[far(step)],
+                device_id={"dp": far(step)}, device_id_type=MESH).wait_recv()
+        for at in range(half_heads):
+            chosen = jnp.zeros((rows, HEAD_SIZE), jnp.float32)
+            for i in range(beams):
+                chosen = jnp.where(row_parent == i, att_all[i, at].astype(jnp.float32), chosen)
+            att_full[core, at] = chosen.astype(jnp.bfloat16)
+        mate_copy.start()
+
+    out_copy = pltpu.make_async_remote_copy(
+        src_ref=out_send.at[1 - tens], dst_ref=out_recv, send_sem=pair_send_sem.at[2],
+        recv_sem=pair_recv_sem.at[2], device_id=across, device_id_type=MESH)
+    row_count = 2 * beams
+
+    def project():
+        mate_wait.wait_recv()
+        load_weight.wait()
+        pieces = []
+        for k in range(kv_heads):
+            whole = att_full[k // half_heads, k % half_heads].astype(jnp.float32)
+            pieces += [whole[g * row_count:(g + 1) * row_count] for g in range(rows // row_count)]
+        flat = jnp.concatenate(pieces, axis=1).astype(jnp.bfloat16)
+        tile = 256
+
+        def column(j, _):
+            lanes = pl.ds(pl.multiple_of(j * tile, tile), tile)
+            term = jnp.dot(flat, held_weight[:, lanes], preferred_element_type=jnp.float32)
+            share = row_count // 2
+            out_send[0, :, lanes] = term[:share]
+            out_send[1, :, lanes] = term[share:]
+            return 0
+
+        lax.fori_loop(0, held_weight.shape[1] // tile, column, 0)
+        out_copy.start()
+
+    queries_ready()
+    head((1 - core) * half_heads, part_send.at[0], 0)
+    serves(0, 1)
+    head((1 - core) * half_heads + 1, part_send.at[0], 1)
+    part_copy.start()
+    serves(1, 2)
+    head(core * half_heads, part_send.at[1], 0)
+    serves(2, 3)
+    head(core * half_heads + 1, part_send.at[1], 1)
+    serves(3, 4)
+    merge()
+    serves(4, 9)
+    pick()
+    serves(9, 11)
+    project()
+    serves(11, CHUNKS + 1)
+    out_copy.wait_recv()
+    out[...] = (out_send[tens] + out_recv[...]).astype(jnp.bfloat16)
+    need_copy.wait_recv()
+    second[...] = jnp.maximum(need_send[...], need_recv[...])
+
+    def drain(c, _):
+        pltpu.make_async_copy(moved_buf.at[c], moved.at[c], moved_sem.at[c]).wait()
+
+        @pl.when(middle)
+        def _():
+            pltpu.make_async_copy(spare_buf.at[c], spare.at[c], spare_sem.at[c]).wait()
+
+        @pl.when(me < beams - 1)
+        def _():
+            right_copy(c, to_right).wait_send()
+
+        @pl.when(me > 0)
+        def _():
+            left_copy(c, to_left).wait_send()
+
+        return 0
+
+    lax.fori_loop(0, CHUNKS, drain, 0)
+    for step in (1, 2, 3):
+        q_copy(step).wait_send()
+        att_copy(step).wait_send()
+    part_copy.wait_send()
+    mate_copy.wait_send()
+    out_copy.wait_send()
+    need_copy.wait_send()
+
+
+def four_beams(cache, query, fresh_key_values, parents, lengths, page_table, out_weight):
+    _, halves, pages, page_len, kv_width = cache.shape
+    kv_heads = kv_width // HEAD_SIZE
+    groups = query.shape[2] // kv_width
+    chunk_shape = (CHUNKS, halves * pages * page_len // CHUNKS, kv_width)
+    q_part = query.reshape(2, kv_heads, groups, HEAD_SIZE).transpose(1, 2, 0, 3)
+    q_part = q_part.reshape(kv_heads, groups * 2, HEAD_SIZE)
+    fresh_part = fresh_key_values.reshape(4, kv_heads, HEAD_SIZE).transpose(1, 0, 2)
+    qf = jnp.concatenate(
+        [q_part, jnp.pad(fresh_part, ((0, 0), (0, 12), (0, 0)))], axis=1)
+    rows = 4 * 16
+    out_rows, out_columns = 4, out_weight.shape[1]
+    vmem = pltpu.VMEM
+    half_heads = kv_heads // 2
+    big = vmem(chunk_shape, jnp.bfloat16)
+    dma = pltpu.SemaphoreType.DMA
+    smem_spec = pl.BlockSpec(memory_space=pltpu.SMEM)
+    vmem_spec = pl.BlockSpec(memory_space=pltpu.VMEM)
+    any_spec = pl.BlockSpec(memory_space=pl.ANY)
+    moved, spare, second, out = pl.pallas_call(
+        chain_kernel,
+        out_shape=[
+            jax.ShapeDtypeStruct(chunk_shape, jnp.bfloat16),
+            jax.ShapeDtypeStruct(chunk_shape, jnp.bfloat16),
+            jax.ShapeDtypeStruct((8, 128), jnp.int32),
+            jax.ShapeDtypeStruct((out_rows, out_columns), jnp.bfloat16),
+        ],
+        in_specs=[smem_spec, smem_spec, smem_spec, vmem_spec, any_spec, any_spec],
+        out_specs=[any_spec, any_spec, vmem_spec, vmem_spec],
+        scratch_shapes=[
+            big, big, big, big, big, big, big,
+            vmem(out_weight.shape, jnp.bfloat16),
+            vmem((4, kv_heads, 32, HEAD_SIZE), jnp.bfloat16),
+            vmem((kv_heads, rows, HEAD_SIZE), jnp.bfloat16),
+            vmem((2, half_heads, 2, rows, HEAD_SIZE), jnp.float32),
+            vmem((half_heads, 2, rows, HEAD_SIZE), jnp.float32),
+            vmem((4, half_heads, rows, HEAD_SIZE), jnp.bfloat16),
+            vmem((2, half_heads, rows, HEAD_SIZE), jnp.bfloat16),
+            vmem((2, out_rows, out_columns), jnp.float32),
+            vmem((out_rows, out_columns), jnp.float32),
+            vmem((8, 128), jnp.int32),
+            vmem((8, 128), jnp.int32),
+            dma, dma,
+            dma((CHUNKS,)), dma((CHUNKS,)), dma((CHUNKS,)), dma((CHUNKS,)),
+            dma((CHUNKS,)), dma((CHUNKS,)),
+            dma((4,)), dma((4,)), dma((4,)), dma((4,)), dma((4,)), dma((4,)),
+        ],
+        compiler_params=pltpu.CompilerParams(
+            collective_id=0, has_side_effects=True, vmem_limit_bytes=48 * 1024 * 1024),
+        name="chain",
+    )(parents, lengths, page_table, qf, cache.reshape(chunk_shape), out_weight)
+
+    here = lax.axis_index("dp")
+    low = (parents[2] < 2) & (parents[3] < 2) & (parents[2] != parents[3]) & (here == 2)
+    high = (parents[0] > 1) & (parents[1] > 1) & (parents[0] != parents[1]) & (here == 1)
+
+    def again(first, payload):
+        arrived = lax.ppermute(payload, "dp", [(1, 2), (2, 1)])
+        return jnp.where(low | high, arrived, first)
+
+    moved = lax.cond(second[0, 0] > 0, again, lambda first, payload: first, moved, spare)
+    return (moved.reshape(cache.shape), out)
+
+
 def solution(mesh):
     in_specs = (
         P(("groups", "dp"), None, "seq", None, "tensor"),
@@ -144,6 +537,8 @@
         P(("groups", "dp"), None, "seq", None, "tensor"),
         P(("groups", "tensor"), ("dp", "seq")),
     )
+    sizes = tuple(mesh.shape[axis] for axis in ("groups", "dp", "tensor", "seq"))
+    body = four_beams if sizes == (2, 4, 2, 2) else per_device
     return jax.shard_map(
-        per_device, mesh=mesh, in_specs=in_specs, out_specs=out_specs, check_vma=False
-    )
+        body, mesh=mesh, in_specs=in_specs, out_specs=out_specs, check_vma=False
+    )

time: 212 us -> 127 us (0.60)
  the two profiles are of different devices: /device:TPU:0 before, /device:TPU:14 now
where the time goes in v1:
time: 127 us; the launch traced here: 126 us
  Pallas kernels  72.8 us (57%)
  waiting for transfers between devices  37.2 us (29%)
  local copies, waits for them, and re-layouts  6.72 us (5%)
  loops' own time  4.9 us (4%)
  starting transfers between devices  1.92 us (2%)
  between operations  1.31 us (1%)
  other arithmetic  1.27 us (1%)
    pallas_call x1, Pallas kernels, four_beams(): pl.pallas_call(chain_kernel, out_shape=[jax.ShapeDtypeStruct(chunk_shape,...  72.8 us
    ppermute x1, waiting for transfers between devices, again(): arrived = lax.ppermute(payload, 'dp', [(1, 2), (2, 1)])  37.2 us
    another operation x1, loops' own time, four_beams(): lax.cond(second[0, 0] > 0, again, lambda first, payload: first, moved, sp...  4.9 us
    unnamed x10, local copies, waits for them, and re-layouts  4.85 us
  transfers between devices with their start and end apart: 1, of which 1 were waited for; matrix products, arithmetic and copies ran while one was open for 1% of the time, Pallas kernels for 0%

profile of v1, /device:TPU:14, one launch (start us, length us, event | category | flops | bytes accessed | tf_op | source)
XLA Modules:
  0.0 126.1 jit_solution(1061911934379342014)
XLA Ops:
  0.6 0.7 reshape.45
  1.3 0.7 fusion.1.qf
  2.1 0.0 copy-start
  2.1 1.6 %copy-done = bf16[1,2,4,256,512]{4,3,2,1,0:T(8,128)(2,1)S(1)} copy-done((bf16[1,2,4,256,512]{4,3,2,1,0:T(8,128)(2,1)S(1)}, bf16[1,2,4,256,512]{4,3,2,1,0:T(8,128)(2,1)}, u32[]{:S(2)}) %copy-start) | copy-done | bytes 2097176
  3.7 0.0 copy-start.1
  3.7 0.7 copy-done.1
  4.3 0.0 copy-start.2
  4.3 0.7 copy-done.2
  5.0 0.0 copy-start.3
  5.0 72.8 %chain.1 = (bf16[16,128,512]{2,1,0:T(8,128)(2,1)S(1)}, bf16[16,128,512]{2,1,0:T(8,128)(2,1)}, s32[8,128]{1,0:T(8,128)S(1)}, bf16[4,1024]{1,0:T(4,128)(2,1)S(1)}) custom-call(s32[4]{0:T(128)} %parents.1, s32[4]{0:T(128)S(1)} %copy-done.2, s32[4,8]{1,0:T(4,128)S(1)} %copy-done.1, bf16[4,32,128]{2,1,0:T(8,128)(2,1)S(1)} %fusion.1.qf, ...), custom_call_target="tpu_custom_call" | custom-call | tf_op jit(solution)/shard_map/chain/pallas_call | solution.py:481
  77.8 0.5 slice.23
  78.9 0.0 copy-done.3
  78.9 45.2 %conditional.1 = (bf16[16,128,512]{2,1,0:T(8,128)(2,1)S(1)}) conditional(s32[]{:T(128)} %bitcast.7, bf16[16,128,512]{2,1,0:T(8,128)(2,1)S(1)} %get-tuple-element.65, (s32[4]{0:T(128)S(1)}, s32[]{:T(128)}, bf16[16,128,512]{2,1,0:T(8,128)(2,1)}, bf16[16,128,512]{2,1,0:T(8,128)(2,1)S(1)}) %tuple.62), branch_computations={%region_0.1_spmd, %region_1.2_spmd} | conditional | flops 1048591 | bytes 14680238 | solution.py:522
  78.9 1.9 %collective-permute-start = (bf16[16,128,512]{2,1,0:T(8,128)(2,1)}, bf16[16,128,512]{2,1,0:T(8,128)(2,1)}, u32[]{:S(2)}, u32[]{:S(2)}) collective-permute-start(bf16[16,128,512]{2,1,0:T(8,128)(2,1)} %get-tuple-element.56), channel_id=1, source_target_pairs={{4,8},{8,4},{5,9},{9,5},{6,10},{10,6},{7,11},{11,7},{20,24},{24,20... | collective-permute-start | bytes 6291464 | tf_op jit(solution)/shard_map/cond/branch_1_fun/ppermute | solution.py:519
  80.9 0.7 fusion.2
  86.4 37.2 %collective-permute-done = bf16[16,128,512]{2,1,0:T(8,128)(2,1)} collective-permute-done((bf16[16,128,512]{2,1,0:T(8,128)(2,1)}, bf16[16,128,512]{2,1,0:T(8,128)(2,1)}, u32[]{:S(2)}, u32[]{:S(2)}) %collective-permute-start) | collective-permute-done | bytes 2097184 | tf_op jit(solution)/shard_map/cond/branch_1_fun/ppermute | solution.py:519
  123.6 0.5 broadcast_select_fusion
  124.2 1.3 %copy.18 = bf16[1,2,4,256,512]{4,3,2,1,0:T(8,128)(2,1)} copy(bf16[1,2,4,256,512]{4,3,2,1,0:T(8,128)(2,1)S(1)} %bitcast.14) | data formatting | bytes 4194304
  125.5 0.6 copy.19
  (1 shorter events, 0.0 us)
Async XLA Ops:
  2.1 1.6 %copy-start = (bf16[1,2,4,256,512]{4,3,2,1,0:T(8,128)(2,1)S(1)}, bf16[1,2,4,256,512]{4,3,2,1,0:T(8,128)(2,1)}, u32[]{:S(2)}) copy-start(bf16[1,2,4,256,512]{4,3,2,1,0:T(8,128)(2,1)} %param.9) | copy-start | bytes 6291460
  3.7 0.7 copy-start.1
  4.3 0.7 copy-start.2
  5.0 73.9 %copy-start.3 = (s32[4]{0:T(128)S(1)}, s32[4]{0:T(128)}, u32[]{:S(2)}) copy-start(s32[4]{0:T(128)} %parents.1) | copy-start | bytes 52
  78.9 44.7 %collective-permute-start = (bf16[16,128,512]{2,1,0:T(8,128)(2,1)}, bf16[16,128,512]{2,1,0:T(8,128)(2,1)}, u32[]{:S(2)}, u32[]{:S(2)}) collective-permute-start(bf16[16,128,512]{2,1,0:T(8,128)(2,1)} %get-tuple-element.56), channel_id=1, source_target_pairs={{4,8},{8,4},{5,9},{9,5},{6,10},{10,6},{7,11},{11,7},{20,24},{24,20... | collective-permute-start | bytes 6291464 | tf_op jit(solution)/shard_map/cond/branch_1_fun/ppermute | solution.py:519
